TPU v7x, 32 devices: a whole 2x2x4 slice. The times are simulated.
32 devices in a mesh: groups: 2 (over y), feat: 4 (over z), dp: 2 (over x), rep: 2 (over core).
Axes of the slice: x: 2, y: 2, z: 4, core: 2. Of those that a mesh axis runs over, the one named last changes fastest.
Arguments:
- features: bfloat16 [8, 4096, 768], P(('groups', 'dp', 'rep'), None, 'feat'), parts along dimension 0, may hold values from -6 to 6
- self_ids: int32 [8, 512], P(('groups', 'dp', 'rep')), parts along dimension 0, may hold values from 0 to 4095
- first_dst: int32 [8, 6], P(('groups', 'dp', 'rep')), parts along dimension 0, may hold values from 0 to 3
- first_src: int32 [8, 6], P(('groups', 'dp', 'rep')), parts along dimension 0, may hold values from 0 to 31
- first_words: int32 [8, 6, 5, 128], P(('groups', 'dp', 'rep')), parts along dimension 0, may hold values from 0 to 1073741823, as said below
- second_dst: int32 [8, 5, 1], P(('groups', 'dp', 'rep')), parts along dimension 0, may hold values from 0 to 3; in each aligned block of 5 rows (0 to 4, 5 to 9, ..., all dimensions but the last counted through in order) at most 4 rows name the same one
- second_src: int32 [8, 5], P(('groups', 'dp', 'rep')), parts along dimension 0, may hold values from 0 to 3
- second_words: int32 [8, 5, 5, 128], P(('groups', 'dp', 'rep')), parts along dimension 0, may hold values from 0 to 1073741823, as said below
- w1_self: bfloat16 [768, 1024], P('feat'), may hold values from -0.21875 to 0.21875
- w1_neigh: bfloat16 [768, 1024], P('feat'), may hold values from -0.21875 to 0.21875
- bias_one: float32 [1024], replicated, may hold values from -3 to 3
- w2_self: bfloat16 [1024, 153], replicated, may hold values from -0.1875 to 0.1875
- w2_neigh: bfloat16 [1024, 153], replicated, may hold values from -0.1875 to 0.1875
- bias_two: float32 [153], replicated, may hold values from -3 to 3
- cotangent: float32 [8, 512, 153], P(('groups', 'dp', 'rep'), 'feat'), parts along dimension 0, may hold values from -0.06 to 0.06
Outputs:
- logits: float32 [8, 512, 153], P(('groups', 'dp', 'rep'), 'feat'), parts along dimension 0
- grad_self: float32 [2048, 153], P('groups'), parts along dimension 0
- grad_neigh: float32 [2048, 153], P('groups'), parts along dimension 0
There are 2 independent parts, one for each index of `groups`. A program takes and returns all parts, laid end to end along the dimension named above; an argument that names none is the same for every part. Nothing has to cross between parts.
Inputs may be any that keep to these rules, and one draw needn't show every extreme that they name: `first_words`: bits for destination rows 128 and above (word 4, bits 8 to 29) are zero. `second_words`: bits for destination rows 128 and above (word 4, bits 8 to 29) are zero. `second_dst`: among the 5 tiles of one slot no destination block is named more than 4 times; in some slot a block is named exactly 4 times.
All inputs are finite; a program needn't handle non-finite values.
Results may differ from a plain program's by a relative error of at most 0.01.
Values may be sent and summed in bfloat16 or wider, within the bound.
A program may use at most 64 MiB of HBM per device.

v0:
```python
import jax
import jax.numpy as jnp
from jax import lax
from jax.sharding import PartitionSpec as P

BLK = 128
TMAX2 = 4


highest = lax.Precision.HIGHEST


def unpack_ints(packed_words):
    shifts = jnp.arange(30, dtype=jnp.int32)
    bit_table = jnp.right_shift(packed_words[:, :, None, :], shifts[None, None, :, None]) & 1
    bit_table = bit_table.reshape(
        packed_words.shape[0], packed_words.shape[1] * 30, packed_words.shape[2]
    )
    return bit_table[:, :BLK, :]


def body(
    features,
    self_ids,
    first_dst,
    first_src,
    first_words,
    second_dst,
    second_src,
    second_words,
    w1_self,
    w1_neigh,
    bias_one,
    w2_self,
    w2_neigh,
    bias_two,
    cotangent,
):
    feature_rows = features[0]
    columns = feature_rows.shape[1]
    feat_size = lax.axis_size("feat")
    position = lax.axis_index("feat")
    first_ints = unpack_ints(first_words[0])
    first_masks = first_ints.astype(jnp.bfloat16)
    source_count = feature_rows.shape[0] // BLK
    source_blocks = feature_rows.reshape(source_count, BLK, columns)[first_src[0]]
    products = jnp.einsum(
        "trs,tsw->trw", first_masks, source_blocks, preferred_element_type=jnp.float32
    )
    onehot_dst = (first_dst[0][:, None] == jnp.arange(feat_size, dtype=jnp.int32)[None, :]).astype(
        jnp.float32
    )
    totals = jnp.einsum("td,trw->drw", onehot_dst, products, precision=highest).reshape(
        feat_size * BLK, columns
    )
    row_ones = jnp.sum(first_ints, axis=2).astype(jnp.float32)
    degree = jnp.einsum("td,tr->dr", onehot_dst, row_ones, precision=highest).reshape(
        feat_size * BLK
    )
    first_mean = (totals / jnp.maximum(degree, 1.0)[:, None]).astype(jnp.bfloat16)
    self_feats = feature_rows[self_ids[0]]
    summed = lax.psum_scatter(
        (
            jnp.dot(self_feats, w1_self, preferred_element_type=jnp.float32)
            + jnp.dot(first_mean, w1_neigh, preferred_element_type=jnp.float32)
        ).astype(jnp.bfloat16),
        "feat",
        scatter_dimension=0,
        tiled=True,
    ).astype(jnp.float32)
    hidden_own = jax.nn.relu(summed + bias_one).astype(jnp.bfloat16)
    dst_two = second_dst[0][:, 0]
    tile_total = dst_two.shape[0]
    is_own = dst_two == position
    sort_keys = jnp.where(is_own, 0, 1).astype(jnp.int32) * tile_total + jnp.arange(
        tile_total, dtype=jnp.int32
    )
    tile_order = jnp.argsort(sort_keys)[:TMAX2]
    chosen = is_own[tile_order].astype(jnp.float32)
    chosen_src = second_src[0][tile_order]
    own_masks = unpack_ints(second_words[0][tile_order]).astype(jnp.float32) * chosen[:, None, None]
    degree_two = jnp.maximum(jnp.sum(own_masks, axis=(0, 2)), 1.0)
    cot_rows = cotangent[0]
    hidden_all = lax.all_gather(hidden_own, "feat", axis=0, tiled=True)
    blocks_two = hidden_all.reshape(feat_size, BLK, -1)[chosen_src]
    totals_two = jnp.einsum(
        "trs,tsh->rh",
        own_masks.astype(jnp.bfloat16),
        blocks_two,
        preferred_element_type=jnp.float32,
    )
    second_mean = totals_two / degree_two[:, None]
    neigh_out = jnp.dot(second_mean, w2_neigh.astype(jnp.float32), precision=highest)
    grad_neigh = jnp.dot(second_mean.T, cot_rows, precision=highest)
    logits = jnp.dot(hidden_own, w2_self, preferred_element_type=jnp.float32) + neigh_out + bias_two
    grad_self = jnp.dot(hidden_own.astype(jnp.float32).T, cot_rows, precision=highest)
    grad_self, grad_neigh = lax.psum((grad_self, grad_neigh), ("feat", "dp", "rep"))
    return (logits[None], grad_self, grad_neigh)


def solution(mesh):
    placed = (
        P(("groups", "dp", "rep"), None, "feat"),
        P(("groups", "dp", "rep"), None),
        P(("groups", "dp", "rep"), None),
        P(("groups", "dp", "rep"), None),
        P(("groups", "dp", "rep"), None, None, None),
        P(("groups", "dp", "rep"), None, None),
        P(("groups", "dp", "rep"), None),
        P(("groups", "dp", "rep"), None, None, None),
        P("feat", None),
        P("feat", None),
        P(),
        P(),
        P(),
        P(),
        P(("groups", "dp", "rep"), "feat", None),
    )
    return jax.shard_map(
        body,
        mesh=mesh,
        in_specs=placed,
        out_specs=(P(("groups", "dp", "rep"), "feat", None), P("groups", None), P("groups", None)),
        check_vma=False,
    )
```

profile of v0, /device:TPU:0, one launch (start us, length us, event | category | flops | bytes accessed | tf_op | source)
XLA Modules:
  0.0 189.6 jit_solution(10908344297618989884)
XLA Ops:
  7.2 0.0 copy-start
  7.2 0.0 reduce-scatter.2.cloned.1.call-start
  7.2 0.1 shift_right_arithmetic.46
  7.3 0.7 copy.55
  8.1 3.2 %copy.26 = bf16[1,4096,192]{2,1,0:T(8,128)(2,1)S(1)} copy(bf16[1,4096,192]{1,2,0:T(8,128)(2,1)} %param.15) | data formatting | bytes 3145728 | tf_op args[0]
  11.3 1.7 copy.37
  13.0 0.0 copy-start.13
  13.0 0.0 copy-start.9
  13.1 1.8 copy.29
  14.8 2.0 %gather_fusion.1 = bf16[6,128,192]{1,2,0:T(8,128)(2,1)S(1)} fusion(bf16[32,128,192]{1,2,0:T(8,128)(2,1)} %copy.29, s32[1024]{0:T(1024)S(1)} %pad_clamp_fusion.2), kind=kCustom, calls=%fused_computation.1 | custom fusion | bytes 589848 | tf_op jit(solution)/shard_map/gather | solution.py:46
  16.9 0.2 fusion.9
  17.1 0.3 fusion.13
  17.4 0.8 fusion.4
  18.2 0.1 fusion.2
  18.4 0.0 copy-start.3
  18.4 2.0 %gather_fusion = bf16[512,192]{1,0:T(8,128)(2,1)S(1)} fusion(bf16[4096,192]{1,0:T(8,128)(2,1)S(1)} %bitcast.67, s32[1024]{0:T(1024)S(1)} %pad_clamp_fusion.3), kind=kCustom, calls=%fused_computation | custom fusion | bytes 395264 | tf_op jit(solution)/shard_map/gather | solution.py:61
  20.4 0.5 fusion.15
  20.9 0.0 copy-start.8
  20.9 0.0 copy-start.12
  20.9 0.0 copy-start.1
  20.9 1.4 add_convert_fusion
  22.3 0.0 reduce-scatter.2.cloned.1.call-update
  22.3 0.0 all-gather.2.cloned.1.call-start
  22.4 29.9 %reduce-scatter.2.cloned.1.call-done = bf16[128,1024]{1,0:T(8,128)(2,1)} async-done(((bf16[512,1024]{1,0:T(8,128)(2,1)}), bf16[128,1024]{1,0:T(8,128)(2,1)}) %reduce-scatter.2.cloned.1.call-update) | async-done | bytes 262160 | tf_op jit(solution)/shard_map/reduce_scatter | solution.py:62
  52.3 1.7 maximum_convert_fusion
  54.0 0.0 all-gather.2.cloned.1.call-update
  54.1 0.0 all-reduce.3.cloned.1.call-start
  54.1 1.0 sort.17
  55.1 0.0 copy-done.1
  55.1 0.6 gather_fusion.4
  55.8 0.6 gather_fusion.3
  56.4 0.6 gather_fusion.2
  57.1 1.9 fusion.21
  59.0 1.2 fusion.25
  60.2 20.9 %all-gather.2.cloned.1.call-done = bf16[512,1024]{1,0:T(8,128)(2,1)} async-done(((bf16[128,1024]{1,0:T(8,128)(2,1)}), bf16[512,1024]{1,0:T(8,128)(2,1)}) %all-gather.2.cloned.1.call-update) | async-done | bytes 1048592 | tf_op jit(solution)/shard_map/all_gather | solution.py:84
  81.2 1.8 gather_fusion.5
  83.0 0.0 copy-start.6
  83.0 0.3 fusion.3
  83.3 0.0 copy-start.5
  83.3 0.0 copy-start.11
  83.4 1.5 fusion.23
  84.9 0.0 all-reduce.3.cloned.1.call-update
  84.9 0.2 fusion.37
  85.2 0.5 fusion.1
  85.7 0.7 copy.33
  86.4 92.7 %all-reduce.3.cloned.1.call-done = (f32[1024,153]{0,1:T(8,128)}, f32[1024,153]{0,1:T(8,128)}) async-done(((f32[1024,153]{0,1:T(8,128)}, f32[1024,153]{0,1:T(8,128)}), (f32[1024,153]{0,1:T(8,128)}, f32[1024,153]{0,1:T(8,128)})) %all-reduce.3.cloned.1.call-update) | async-done | bytes 1253392 | tf_op jit(solution)/shard_map/psum | solution.py:97
  179.1 2.0 %copy.59 = f32[1024,153]{0,1:T(8,128)} copy(f32[1024,153]{0,1:T(8,128)} %get-tuple-element.21) | data formatting | bytes 1253376
  181.1 2.0 %copy.60 = f32[1024,153]{0,1:T(8,128)} copy(f32[1024,153]{0,1:T(8,128)} %get-tuple-element.22) | data formatting | bytes 1253376
  (36 shorter events, 0.2 us)
Async XLA Ops:
  7.2 13.2 %copy-start = (bf16[192,1024]{1,0:T(8,128)(2,1)S(1)}, bf16[192,1024]{1,0:T(8,128)(2,1)}, u32[]{:S(2)}) copy-start(bf16[192,1024]{1,0:T(8,128)(2,1)} %param.24) | copy-start | bytes 1179652
  7.2 45.1 %reduce-scatter.2.cloned.1.call-start = ((), (), s32[]{:S(2)}) async-start(), calls=%async_computation.1 | async-start | bytes 1310720 | tf_op jit(solution)/shard_map/reduce_scatter | solution.py:62
  13.0 1.8 copy-start.13
  13.0 4.4 %copy-start.9 = (s32[1,6]{1,0:T(1,128)S(1)}, s32[1,6]{1,0:T(1,128)}, u32[]{:S(2)}) copy-start(s32[1,6]{1,0:T(1,128)} %param.17) | copy-start | bytes 76
  14.8 3.5 %copy-start.10 = (s32[1,512]{1,0:T(1,128)S(1)}, s32[1,512]{1,0:T(1,128)}, u32[]{:S(2)}) copy-start(s32[1,512]{1,0:T(1,128)} %param.16) | copy-start | bytes 6148
  18.4 2.5 %copy-start.3 = (bf16[192,1024]{1,0:T(8,128)(2,1)S(1)}, bf16[192,1024]{1,0:T(8,128)(2,1)}, u32[]{:S(2)}) copy-start(bf16[192,1024]{1,0:T(8,128)(2,1)} %param.23) | copy-start | bytes 1179652
  20.9 31.5 %copy-start.8 = (f32[1024]{0:T(1024)S(1)}, f32[1024]{0:T(1024)}, u32[]{:S(2)}) copy-start(f32[1024]{0:T(1024)} %param.25) | copy-start | bytes 12292
  20.9 33.2 %copy-start.12 = (s32[1,5,1]{1,2,0:T(1,128)S(1)}, s32[1,5,1]{1,2,0:T(1,128)}, u32[]{:S(2)}) copy-start(s32[1,5,1]{1,2,0:T(1,128)} %param.20) | copy-start | bytes 64
  20.9 34.2 %copy-start.1 = (s32[1,5]{1,0:T(1,128)S(1)}, s32[1,5]{1,0:T(1,128)}, u32[]{:S(2)}) copy-start(s32[1,5]{1,0:T(1,128)} %param.21) | copy-start | bytes 64
  22.3 34.1 %copy-start.7 = (s32[1,5,5,128]{3,0,2,1:T(1,128)S(1)}, s32[1,5,5,128]{3,0,2,1:T(1,128)}, u32[]{:S(2)}) copy-start(s32[1,5,5,128]{3,0,2,1:T(1,128)} %param.22) | copy-start | bytes 38404
  22.3 36.7 %copy-start.4 = (f32[1,128,153]{1,0,2:T(1,128)S(1)}, f32[1,128,153]{1,0,2:T(1,128)}, u32[]{:S(2)}) copy-start(f32[1,128,153]{1,0,2:T(1,128)} %param.29) | copy-start | bytes 235012
  22.3 58.8 %all-gather.2.cloned.1.call-start = ((), (), s32[]{:S(2)}) async-start(), calls=%async_computation.2 | async-start | bytes 1310720 | tf_op jit(solution)/shard_map/all_gather | solution.py:84
  54.0 5.0 %copy-start.2 = (bf16[128,1024]{1,0:T(8,128)(2,1)S(1)}, bf16[128,1024]{1,0:T(8,128)(2,1)}, u32[]{:S(2)}) copy-start(bf16[128,1024]{1,0:T(8,128)(2,1)} %maximum_convert_fusion) | copy-start | bytes 786436
  54.1 125.1 %all-reduce.3.cloned.1.call-start = ((), (), s32[]{:S(2)}) async-start(), calls=%async_computation.3 | async-start | bytes 2621440 | tf_op jit(solution)/shard_map/psum | solution.py:97
  83.0 1.9 %copy-start.6 = (bf16[1024,153]{0,1:T(8,128)(2,1)S(1)}, bf16[1024,153]{0,1:T(8,128)(2,1)}, u32[]{:S(2)}) copy-start(bf16[1024,153]{0,1:T(8,128)(2,1)} %param.26) | copy-start | bytes 940036
  83.3 1.9 copy-start.5
  83.3 1.9 copy-start.11
Sparse Core Ops, SparseCore 0:
  22.4 29.8 reduce-scatter.1
  54.5 26.5 all-gather.1
  85.7 93.3 all-reduce.2
where the time goes:
time: 190 us
  waiting for transfers between devices  144 us (76%)
  local copies, waits for them, and re-layouts  20 us (11%)
  between operations  14.1 us (7%)
  matrix products  6.93 us (4%)
  other arithmetic  4.88 us (3%)
    psum x1, waiting for transfers between devices, body(): lax.psum((grad_self, grad_neigh), ('feat', 'dp', 'rep'))  92.7 us
    reduce_scatter x1, waiting for transfers between devices, body(): lax.psum_scatter((jnp.dot(self_feats, w1_self, preferred_element_type=jnp...  29.9 us
    all_gather x1, waiting for transfers between devices, body(): hidden_all = lax.all_gather(hidden_own, 'feat', axis=0, tiled=True)  20.9 us
    unnamed x34, local copies, waits for them, and re-layouts  9.67 us
  transfers between devices with their start and end apart: 3, of which 3 were waited for; matrix products, arithmetic and copies ran while one was open for 4% of the time, Pallas kernels for 0%

commit v1 on v0

v1 whole, which is shorter than its diff:
```python
import functools

import jax
import jax.numpy as jnp
from jax import lax
from jax.experimental import pallas as pl
from jax.experimental.pallas import tpu as pltpu
from jax.sharding import PartitionSpec as P

BLK = 128
WORD = 30
MESH = pl.DeviceIdType.MESH
F32 = jnp.float32
BF16 = jnp.bfloat16


def round_up(value, step):
    return -(-value // step) * step


def each(count, step):
    if count <= 4:
        for index in range(count):
            step(index)
    else:
        lax.fori_loop(0, count, lambda index, carry: (step(index), carry)[1], 0)


def partners(me, size):
    if size & (size - 1) == 0:
        return [me ^ k for k in range(size - 1, 0, -1)]
    return [lax.rem(me + k, size) for k in range(1, size)]


def dot(a, b, dims):
    return lax.dot_general(a, b, (dims, ((), ())), preferred_element_type=F32)


NN = ((1,), (0,))
NT = ((1,), (1,))
TN = ((0,), (0,))


def unpack(words, row_word, row_shift):
    spread = jnp.broadcast_to(words[0:1, :], (BLK, BLK))
    for k in range(1, words.shape[0]):
        spread = jnp.where(row_word == k, words[k : k + 1, :], spread)
    return (jnp.right_shift(spread, row_shift) & 1).astype(F32)


def kernel(
    sizes,
    dst1,
    src1,
    dst2,
    src2,
    ids,
    words1,
    words2,
    feats,
    w1s,
    w1n,
    b1,
    w2s,
    w2n,
    cot,
    logits_out,
    grads_out,
    cotg,
    masks1,
    masks2,
    adj1,
    adj2,
    part,
    got,
    w2z,
    lf,
    lsend,
    lgot,
    cg,
    gsend,
    ggot,
    full,
    cot_s,
    cot_r,
    part_s,
    part_r,
    l_s,
    l_r,
    g_s,
    g_r,
    z_s,
    z_r,
    x_s,
    x_r,
    c_s,
    c_r,
):
    nz, nd, nr, hc, classes = sizes
    z = lax.axis_index("feat")
    d = lax.axis_index("dp")
    r = lax.axis_index("rep")
    y = lax.axis_index("groups")
    q = d * nr + r
    planes = nd * nr
    nodes = nz * BLK
    tile1, tile2 = words1.shape[0], words2.shape[0]
    cp = cot.shape[0]
    pc = gsend.shape[1]
    zs = partners(z, nz)
    qs = partners(q, planes)

    def at(zz, qq):
        return (y, zz, qq // nr, lax.rem(qq, nr))

    def remote(src, dst, send, recv, where):
        return pltpu.make_async_remote_copy(
            src_ref=src, dst_ref=dst, send_sem=send, recv_sem=recv, device_id=where, device_id_type=MESH
        )

    barrier = pltpu.get_barrier_semaphore()
    for p in zs:
        pl.semaphore_signal(barrier, inc=1, device_id=at(p, q), device_id_type=MESH)
    for p in qs:
        pl.semaphore_signal(barrier, inc=1, device_id=at(z, p), device_id_type=MESH)
    pl.semaphore_wait(barrier, nz + planes - 2)

    pending = []

    def send(src, dst, s, rv, where):
        copy = remote(src, dst, s, rv, where)
        copy.start()
        pending.append(copy)

    def arrived(dst, s, rv, where):
        remote(dst, dst, s, rv, where).wait_recv()

    for p in zs:
        send(cot, cotg.at[z], cot_s.at[p], cot_r.at[z], at(p, q))
    cotg[z] = cot[...]

    row = lax.broadcasted_iota(jnp.int32, (BLK, BLK), 0)
    row_word = jnp.zeros((BLK, BLK), jnp.int32)
    for k in range(1, words1.shape[1]):
        row_word = row_word + (row >= WORD * k).astype(jnp.int32)
    row_shift = row - WORD * row_word

    for t in range(tile1):
        masks1[t] = unpack(words1[t], row_word, row_shift)

    def fill1(block):
        for t in range(tile1):
            keep = jnp.where(jnp.full((BLK, BLK), dst1[t], jnp.int32) == block, masks1[t], 0.0)
            adj1[pl.ds(pl.multiple_of(block * BLK, BLK), BLK), t * BLK : (t + 1) * BLK] = keep.astype(BF16)

    each(nz, fill1)
    picked = []
    for t in range(tile1):
        wanted = jnp.full((feats.shape[0], BLK), src1[t], jnp.int32)
        block = feats[:, 0:BLK]
        for k in range(1, feats.shape[1] // BLK):
            block = jnp.where(wanted == k, feats[:, k * BLK : (k + 1) * BLK], block)
        picked.append(block)
    picked = jnp.concatenate(picked, axis=1)
    degree = dot(jnp.ones((16, tile1 * BLK), BF16), adj1[...], NT)[0:1, :]
    mean_t = (dot(picked, adj1[...], NT) / jnp.maximum(degree, 1.0)).astype(BF16)
    sources = feats.shape[1]
    chunk = 512
    self_t = None
    for k in range(0, sources, chunk):
        spot = lax.broadcasted_iota(jnp.int32, (chunk, nodes), 0) + k
        onehot = jnp.where(spot == ids[...], 1.0, 0.0).astype(BF16)
        term = dot(feats[:, k : k + chunk], onehot, NN)
        self_t = term if self_t is None else self_t + term
    self_t = self_t.astype(BF16)
    for j in range(nz):
        cols = slice(j * hc, (j + 1) * hc)
        part[j] = (dot(self_t, w1s[:, cols], TN) + dot(mean_t, w1n[:, cols], TN)).astype(BF16)
    for p in zs:
        send(part.at[p], got.at[z], part_s.at[p], part_r.at[z], at(p, q))

    for t in range(tile2):
        masks2[t] = unpack(words2[t], row_word, row_shift)

    def fill2(dst):
        rows = pl.ds(pl.multiple_of(dst * BLK, BLK), BLK)
        kept = [
            jnp.where(jnp.full((BLK, BLK), dst2[t], jnp.int32) == dst, masks2[t], 0.0)
            for t in range(tile2)
        ]
        for src in range(nz):
            count = jnp.zeros((BLK, BLK), F32)
            for t in range(tile2):
                count = count + jnp.where(jnp.full((BLK, BLK), src2[t], jnp.int32) == src, kept[t], 0.0)
            adj2[rows, src * BLK : (src + 1) * BLK] = count.astype(BF16)

    each(nz, fill2)
    degree2 = jnp.maximum(dot(jnp.ones((16, nodes), BF16), adj2[...], NT)[0:1, :], 1.0)
    inverse2 = 1.0 / degree2
    w2z[...] = jnp.zeros_like(w2z)
    if w2s.shape[1] == hc:
        part_w2s, part_w2n, bias = w2s[...], w2n[...], b1[...]
    else:
        mine = pl.ds(pl.multiple_of(z * hc, BLK), hc)
        part_w2s, part_w2n, bias = w2s[:, mine], w2n[:, mine], b1[:, mine]
    w2z[0:classes, :] = part_w2s.astype(F32)
    w2z[cp : cp + classes, :] = part_w2n.astype(F32)
    w2 = w2z[...].astype(BF16)
    for p in zs:
        arrived(cotg.at[p], cot_s.at[p], cot_r.at[p], at(p, q))
    for j in range(nz):
        cols = slice(j * BLK, (j + 1) * BLK)
        cg[0:cp, cols] = cotg[j]
    scaled = (cg[0:cp, :].astype(F32) * inverse2).astype(BF16)
    cg[cp : 2 * cp, :] = dot(scaled, adj2[...], NN).astype(BF16)
    if cg.shape[0] > 2 * cp:
        cg[2 * cp :, :] = jnp.zeros((cg.shape[0] - 2 * cp, nodes), BF16)

    summed = part[z].astype(F32) + bias
    for p in zs:
        arrived(got.at[p], part_s.at[p], part_r.at[p], at(p, q))
        summed = summed + got[p].astype(F32)
    hidden = jnp.maximum(summed, 0.0).astype(BF16)

    grads = dot(cg[...], hidden, NN).astype(BF16)
    for p in range(planes):
        gsend[p] = grads[p * pc : (p + 1) * pc, :]
    for p in qs:
        send(gsend.at[p], ggot.at[q], g_s.at[p], g_r.at[q], at(z, p))

    uv = dot(w2, hidden, NT)
    lf[...] = uv[0:cp, :] + dot(uv[cp:, :].astype(BF16), adj2[...], NT) * inverse2
    for j in range(nz):
        lsend[j] = lf[:, j * BLK : (j + 1) * BLK].astype(BF16)

    total = gsend[q].astype(F32)
    for p in qs:
        arrived(ggot.at[p], g_s.at[p], g_r.at[p], at(z, p))
        total = total + ggot[p].astype(F32)
    full[z, q] = total.astype(BF16)
    for p in zs:
        send(full.at[z, q], full.at[z, q], z_s.at[p], z_r.at[z], at(p, q))
    for p in zs:
        send(lsend.at[p], lgot.at[z], l_s.at[p], l_r.at[z], at(p, q))

    ds = partners(d, nd)
    rs = partners(r, nr)

    def to_core(zz, dd):
        piece = full.at[zz, dd * nr + r]
        for p in rs:
            send(piece, piece, c_s.at[zz, dd, p], c_r.at[zz, dd, r], (y, z, d, p))

    for zz in [z] + zs[::-1]:
        piece = full.at[zz, q]
        if zz is not z:
            arrived(piece, z_s.at[zz], z_r.at[zz], at(zz, q))
        for p in ds:
            send(piece, piece, x_s.at[zz, p], x_r.at[zz, d], (y, z, p, r))
        to_core(zz, d)
    for zz in [z] + zs[::-1]:
        for p in ds:
            arrived(full.at[zz, p * nr + r], x_s.at[zz, p], x_r.at[zz, p], (y, z, p, r))
            to_core(zz, p)

    out = lf[:, pl.ds(pl.multiple_of(z * BLK, BLK), BLK)]
    for p in zs:
        arrived(lgot.at[p], l_s.at[p], l_r.at[p], at(p, q))
        out = out + lgot[p].astype(F32)
    logits_out[...] = out

    for zz in range(nz):
        for dd in range(nd):
            for p in rs:
                arrived(full.at[zz, dd * nr + p], c_s.at[zz, dd, p], c_r.at[zz, dd, p], (y, z, d, p))
    for zz in range(nz):
        for p in range(planes):
            grads_out[p * pc : (p + 1) * pc, zz * hc : (zz + 1) * hc] = full[zz, p]
    for copy in pending:
        copy.wait_send()


def body(nd, nr, *args):
    (features, self_ids, first_dst, first_src, first_words, second_dst, second_src, second_words) = args[:8]
    w1_self, w1_neigh, bias_one, w2_self, w2_neigh, bias_two, cotangent = args[8:]
    nz = lax.axis_size("feat")
    planes = nd * nr
    h, classes = w2_self.shape
    hc = h // nz
    nodes = self_ids.shape[1]
    tile1, tile2 = first_words.shape[1], second_words.shape[1]
    cp = round_up(classes, 16)
    rows = round_up(2 * cp, 16 * planes)
    pc = rows // planes
    cot = jnp.pad(cotangent[0].T.astype(BF16), ((0, cp - classes), (0, 0)))
    w2s, w2n, b1 = w2_self.T, w2_neigh.T, bias_one[None, :]
    if hc % BLK:
        first = lax.axis_index("feat") * hc
        w2s, w2n, b1 = [lax.dynamic_slice_in_dim(a, first, hc, 1) for a in (w2s, w2n, b1)]
    smem = pl.BlockSpec(memory_space=pltpu.SMEM)
    vmem = pl.BlockSpec(memory_space=pltpu.VMEM)
    dma = pltpu.SemaphoreType.DMA
    logits, grads = pl.pallas_call(
        functools.partial(kernel, (nz, nd, nr, hc, classes)),
        out_shape=(jax.ShapeDtypeStruct((cp, BLK), F32), jax.ShapeDtypeStruct((rows, h), BF16)),
        in_specs=[smem] * 4 + [vmem] * 10,
        out_specs=(vmem, vmem),
        scratch_shapes=[
            pltpu.VMEM((nz, cp, BLK), BF16),
            pltpu.VMEM((tile1, BLK, BLK), F32),
            pltpu.VMEM((tile2, BLK, BLK), F32),
            pltpu.VMEM((nodes, tile1 * BLK), BF16),
            pltpu.VMEM((nodes, nodes), BF16),
            pltpu.VMEM((nz, nodes, hc), BF16),
            pltpu.VMEM((nz, nodes, hc), BF16),
            pltpu.VMEM((2 * cp, hc), F32),
            pltpu.VMEM((cp, nodes), F32),
            pltpu.VMEM((nz, cp, BLK), BF16),
            pltpu.VMEM((nz, cp, BLK), BF16),
            pltpu.VMEM((rows, nodes), BF16),
            pltpu.VMEM((planes, pc, hc), BF16),
            pltpu.VMEM((planes, pc, hc), BF16),
            pltpu.VMEM((nz, planes, pc, hc), BF16),
            dma((nz,)),
            dma((nz,)),
            dma((nz,)),
            dma((nz,)),
            dma((nz,)),
            dma((nz,)),
            dma((planes,)),
            dma((planes,)),
            dma((nz,)),
            dma((nz,)),
            dma((nz, nd)),
            dma((nz, nd)),
            dma((nz, nd, nr)),
            dma((nz, nd, nr)),
        ],
        compiler_params=pltpu.CompilerParams(
            collective_id=0, has_side_effects=True, vmem_limit_bytes=60 * 1024 * 1024
        ),
    )(
        first_dst[0],
        first_src[0],
        second_dst[0, :, 0],
        second_src[0],
        self_ids,
        first_words[0],
        second_words[0],
        features[0].T,
        w1_self,
        w1_neigh,
        b1,
        w2s,
        w2n,
        cot,
    )
    logits = logits[:classes].T + bias_two
    grad_self = grads[:classes].astype(F32).T
    grad_neigh = grads[cp : cp + classes].astype(F32).T
    return (logits[None], grad_self, grad_neigh)


def solution(mesh):
    slot = ("groups", "dp", "rep")
    placed = (
        P(slot, None, "feat"),
        P(slot, None),
        P(slot, None),
        P(slot, None),
        P(slot, None, None, None),
        P(slot, None, None),
        P(slot, None),
        P(slot, None, None, None),
        P("feat", None),
        P("feat", None),
        P(),
        P(),
        P(),
        P(),
        P(slot, "feat", None),
    )
    return jax.shard_map(
        functools.partial(body, mesh.shape["dp"], mesh.shape["rep"]),
        mesh=mesh,
        in_specs=placed,
        out_specs=(P(slot, "feat", None), P("groups", None), P("groups", None)),
        check_vma=False,
    )
```

time: 190 us -> 57.6 us (0.30)
  waiting for transfers between devices: 144 us -> 0 us
  Pallas kernels: 0 us -> 48 us
  local copies, waits for them, and re-layouts: 20 us -> 4.88 us
  between operations: 14.1 us -> 0.66 us
  matrix products: 6.93 us -> 0 us
    psum x1 -> x0, waiting for transfers between devices: 92.7 us -> none  [body(): lax.psum((grad_self, grad_neigh), ('feat', 'dp', 'rep'))]
    pallas_call x0 -> x1, Pallas kernels: none -> 48 us  [body(): pl.pallas_call(functools.partial(kernel, (nz, nd, nr, hc, classes)), out_...]
    reduce_scatter x1 -> x0, waiting for transfers between devices: 29.9 us -> none  [body(): lax.psum_scatter((jnp.dot(self_feats, w1_self, preferred_element_type=jnp...]
    all_gather x1 -> x0, waiting for transfers between devices: 20.9 us -> none  [body(): hidden_all = lax.all_gather(hidden_own, 'feat', axis=0, tiled=True)]
    gather x7 -> x0, local copies, waits for them, and re-layouts: 7.64 us -> none  [the longest x1 2.01 us: body(): feature_rows.reshape(source_count, BLK, columns)[first_src[0]]]
    dot_general x10 -> x0, matrix products: 6.93 us -> none  [the longest x1 1.54 us: body(): grad_neigh = jnp.dot(second_mean.T, cot_rows, precision=highest)]
    unnamed x34 -> x5, local copies, waits for them, and re-layouts: 9.67 us -> 2.93 us
    convert_element_type x3 -> x0, other arithmetic: 3.62 us -> none  [the longest x1 1.89 us: body(): own_masks.astype(jnp.bfloat16)]
  transfers between devices with their start and end apart: 3 -> 0, of which waited for: 3 -> 0; matrix products, arithmetic and copies ran while one was open for 4% -> 0% of each run, Pallas kernels for 0% -> 0%
where the time goes in v1:
time: 57.6 us; the launch traced here: 56.8 us
  Pallas kernels  48 us (83%)
  local copies, waits for them, and re-layouts  4.88 us (8%)
  other arithmetic  3.24 us (6%)
  between operations  0.66 us (1%)
    pallas_call x1, Pallas kernels, body(): pl.pallas_call(functools.partial(kernel, (nz, nd, nr, hc, classes)), out_...  48 us
    unnamed x5, local copies, waits for them, and re-layouts  2.93 us
    transpose x1, other arithmetic, body(): grad_neigh = grads[cp:cp + classes].astype(F32).T  2.27 us
    squeeze x1, local copies, waits for them, and re-layouts, body(): first_words[0]  1.32 us

profile of v1, /device:TPU:0, one launch (start us, length us, event | category | flops | bytes accessed | tf_op | source)
XLA Modules:
  0.0 56.8 jit_solution(1843168410394278347)
XLA Ops:
  0.6 1.3 %copy.33 = s32[1,5,5,128]{3,2,0,1:T(8,128)} copy(s32[1,5,5,128]{3,0,2,1:T(1,128)} %param.22) | data formatting | bytes 25600
  2.0 1.3 %copy.32 = s32[1,6,5,128]{3,2,1,0:T(8,128)} copy(s32[1,6,5,128]{3,0,2,1:T(1,128)} %param.19) | data formatting | bytes 30720 | tf_op jit(solution)/shard_map/squeeze | solution.py:348
  3.3 0.9 %copy.31 = bf16[1,128,153]{1,2,0:T(8,128)(2,1)S(1)} copy(f32[1,128,153]{1,0,2:T(1,128)} %param.29) | data formatting | bytes 117504 | tf_op args[14]
  4.2 0.6 %pad.4.cot = bf16[160,128]{1,0:T(8,128)(2,1)} pad(bf16[153,128]{1,0:T(8,128)(2,1)S(1)} %bitcast.33, bf16[]{:T(256)} %constant.2.clone.1), padding=0_7x0_0 | pad | bytes 80130 | tf_op jit(solution)/shard_map/jit(_pad)/pad | solution.py:295
  4.8 0.0 copy-start
  4.8 48.0 %shard_map.166 = (f32[160,128]{1,0:T(8,128)}, bf16[320,1024]{1,0:T(8,128)(2,1)}) custom-call(s32[6]{0:T(128)} %bitcast.37, s32[6]{0:T(128)} %bitcast.38, s32[5]{0:T(128)} %bitcast.39, s32[5]{0:T(128)} %bitcast.40, s32[1,512]{1,0:T(1,128)} %ids.1, s32[6,5,128]{2,1,0:T(8,128)} %bitcast.34, s32[5,5,128]{2,1,0:T(8,128)} %bitcast.35, bf16[192,4096]{1,0:T(8,128)(2,1)} %bitcast.30, ...), custom_call_target="tpu_custom_call" | custom-call | tf_op jit(solution)/shard_map/pallas_call | solution.py:303
  52.8 0.0 copy-done
  52.8 1.0 %add_bitcast_fusion = f32[1,128,153]{1,2,0:T(8,128)S(1)} fusion(f32[160,128]{1,0:T(8,128)} %get-tuple-element.5, f32[153]{0:T(256)S(1)} %copy-done), kind=kLoop, calls=%fused_computation.3 | loop fusion | flops 19584 | bytes 157284 | tf_op jit(solution)/shard_map/broadcast_in_dim | solution.py:361
  53.8 0.7 %copy.23 = f32[1,128,153]{1,0,2:T(1,128)} copy(f32[1,128,153]{1,2,0:T(8,128)S(1)} %add_bitcast_fusion) | data formatting | bytes 156672
  54.5 2.3 %convert_bitcast_fusion = (f32[1024,153]{0,1:T(8,128)}, f32[1024,153]{0,1:T(8,128)}) fusion(bf16[320,1024]{1,0:T(8,128)(2,1)} %get-tuple-element.6), kind=kLoop, calls=%fused_computation | loop fusion | flops 313344 | bytes 1880064 | tf_op jit(solution)/shard_map/transpose | solution.py:360
Async XLA Ops:
  4.8 48.0 %copy-start = (f32[153]{0:T(256)S(1)}, f32[153]{0:T(256)}, u32[]{:S(2)}) copy-start(f32[153]{0:T(256)} %param.28) | copy-start | bytes 1840

commit v2 on v1

--- a/solution.py
+++ b/solution.py
@@ -42,9 +42,9 @@
 
 
 def unpack(words, row_word, row_shift):
-    spread = jnp.broadcast_to(words[0:1, :], (BLK, BLK))
-    for k in range(1, words.shape[0]):
-        spread = jnp.where(row_word == k, words[k : k + 1, :], spread)
+    spread = jnp.broadcast_to(words[0], (BLK, BLK))
+    for k in range(1, len(words)):
+        spread = jnp.where(row_word == k, words[k], spread)
     return (jnp.right_shift(spread, row_shift) & 1).astype(F32)
 
 
@@ -63,10 +63,12 @@
     b1,
     w2s,
     w2n,
+    b2,
     cot,
     logits_out,
     grads_out,
     cotg,
+    wide,
     masks1,
     masks2,
     adj1,
@@ -104,8 +106,9 @@
     q = d * nr + r
     planes = nd * nr
     nodes = nz * BLK
-    tile1, tile2 = words1.shape[0], words2.shape[0]
-    cp = cot.shape[0]
+    tile1, tile2 = dst1.shape[0], dst2.shape[0]
+    per = words1.shape[0] // tile1
+    cp = cotg.shape[1]
     pc = gsend.shape[1]
     zs = partners(z, nz)
     qs = partners(q, planes)
@@ -123,6 +126,9 @@
         pl.semaphore_signal(barrier, inc=1, device_id=at(p, q), device_id_type=MESH)
     for p in qs:
         pl.semaphore_signal(barrier, inc=1, device_id=at(z, p), device_id_type=MESH)
+    wide[...] = jnp.zeros_like(wide)
+    wide[0:classes, :] = cot[:, 0, :]
+    cotg[z] = wide[...].astype(BF16)
     pl.semaphore_wait(barrier, nz + planes - 2)
 
     pending = []
@@ -136,17 +142,16 @@
         remote(dst, dst, s, rv, where).wait_recv()
 
     for p in zs:
-        send(cot, cotg.at[z], cot_s.at[p], cot_r.at[z], at(p, q))
-    cotg[z] = cot[...]
+        send(cotg.at[z], cotg.at[z], cot_s.at[p], cot_r.at[z], at(p, q))
 
     row = lax.broadcasted_iota(jnp.int32, (BLK, BLK), 0)
     row_word = jnp.zeros((BLK, BLK), jnp.int32)
-    for k in range(1, words1.shape[1]):
+    for k in range(1, per):
         row_word = row_word + (row >= WORD * k).astype(jnp.int32)
     row_shift = row - WORD * row_word
 
     for t in range(tile1):
-        masks1[t] = unpack(words1[t], row_word, row_shift)
+        masks1[t] = unpack([words1[t * per + k] for k in range(per)], row_word, row_shift)
 
     def fill1(block):
         for t in range(tile1):
@@ -180,7 +185,7 @@
         send(part.at[p], got.at[z], part_s.at[p], part_r.at[z], at(p, q))
 
     for t in range(tile2):
-        masks2[t] = unpack(words2[t], row_word, row_shift)
+        masks2[t] = unpack([words2[t * per + k] for k in range(per)], row_word, row_shift)
 
     def fill2(dst):
         rows = pl.ds(pl.multiple_of(dst * BLK, BLK), BLK)
@@ -267,7 +272,9 @@
     for p in zs:
         arrived(lgot.at[p], l_s.at[p], l_r.at[p], at(p, q))
         out = out + lgot[p].astype(F32)
-    logits_out[...] = out
+    wide[...] = out
+    bias_two = jnp.broadcast_to(b2[...], (BLK, classes)).T
+    logits_out[:, 0, :] = wide[0:classes, :] + bias_two
 
     for zz in range(nz):
         for dd in range(nd):
@@ -292,7 +299,7 @@
     cp = round_up(classes, 16)
     rows = round_up(2 * cp, 16 * planes)
     pc = rows // planes
-    cot = jnp.pad(cotangent[0].T.astype(BF16), ((0, cp - classes), (0, 0)))
+    cot = cotangent.transpose(2, 0, 1)
     w2s, w2n, b1 = w2_self.T, w2_neigh.T, bias_one[None, :]
     if hc % BLK:
         first = lax.axis_index("feat") * hc
@@ -302,11 +309,12 @@
     dma = pltpu.SemaphoreType.DMA
     logits, grads = pl.pallas_call(
         functools.partial(kernel, (nz, nd, nr, hc, classes)),
-        out_shape=(jax.ShapeDtypeStruct((cp, BLK), F32), jax.ShapeDtypeStruct((rows, h), BF16)),
-        in_specs=[smem] * 4 + [vmem] * 10,
+        out_shape=(jax.ShapeDtypeStruct((classes, 1, BLK), F32), jax.ShapeDtypeStruct((rows, h), BF16)),
+        in_specs=[smem] * 4 + [vmem] * 11,
         out_specs=(vmem, vmem),
         scratch_shapes=[
             pltpu.VMEM((nz, cp, BLK), BF16),
+            pltpu.VMEM((cp, BLK), F32),
             pltpu.VMEM((tile1, BLK, BLK), F32),
             pltpu.VMEM((tile2, BLK, BLK), F32),
             pltpu.VMEM((nodes, tile1 * BLK), BF16),
@@ -345,20 +353,21 @@
         second_dst[0, :, 0],
         second_src[0],
         self_ids,
-        first_words[0],
-        second_words[0],
+        first_words[0].reshape(-1, 1, BLK),
+        second_words[0].reshape(-1, 1, BLK),
         features[0].T,
         w1_self,
         w1_neigh,
         b1,
         w2s,
         w2n,
+        bias_two[None, :],
         cot,
     )
-    logits = logits[:classes].T + bias_two
+    logits = logits.transpose(1, 2, 0)
     grad_self = grads[:classes].astype(F32).T
     grad_neigh = grads[cp : cp + classes].astype(F32).T
-    return (logits[None], grad_self, grad_neigh)
+    return (logits, grad_self, grad_neigh)
 
 
 def solution(mesh):

time: 57.6 us -> 52.3 us (0.908)
  local copies, waits for them, and re-layouts: 4.88 us -> 0.64 us
  other arithmetic: 3.24 us -> 2.3 us
    unnamed x5 -> x3, local copies, waits for them, and re-layouts: 2.93 us -> 0.64 us
    squeeze x1 -> x0, local copies, waits for them, and re-layouts: 1.32 us -> none  [body(): first_words[0]]
    broadcast_in_dim x1 -> x0, other arithmetic: 0.97 us -> none  [body(): return (logits[None], grad_self, grad_neigh)]
    pad x1 -> x0, local copies, waits for them, and re-layouts: 0.62 us -> none  [body(): cot = jnp.pad(cotangent[0].T.astype(BF16), ((0, cp - classes), (0, 0)))]
where the time goes in v2:
time: 52.3 us; the launch traced here: 51.7 us
  Pallas kernels  48.1 us (92%)
  other arithmetic  2.3 us (4%)
  between operations  0.65 us (1%)
  local copies, waits for them, and re-layouts  0.64 us (1%)
    pallas_call x1, Pallas kernels, body(): pl.pallas_call(functools.partial(kernel, (nz, nd, nr, hc, classes)), out_...  48.1 us
    transpose x1, other arithmetic, body(): grad_neigh = grads[cp:cp + classes].astype(F32).T  2.3 us

profile of v2, /device:TPU:0, one launch (start us, length us, event | category | flops | bytes accessed | tf_op | source)
XLA Modules:
  0.0 51.7 jit_solution(2373564253297743263)
XLA Ops:
  0.6 48.1 %shard_map.166 = (f32[153,1,128]{2,1,0:T(1,128)}, bf16[320,1024]{1,0:T(8,128)(2,1)}) custom-call(s32[6]{0:T(128)} %bitcast.28, s32[6]{0:T(128)} %bitcast.29, s32[5]{0:T(128)} %bitcast.30, s32[5]{0:T(128)} %bitcast.31, s32[1,512]{1,0:T(1,128)} %ids.1, s32[30,1,128]{2,1,0:T(1,128)} %bitcast.24, s32[25,1,128]{2,1,0:T(1,128)} %bitcast.25, ...), custom_call_target="tpu_custom_call" | custom-call | tf_op jit(solution)/shard_map/pallas_call | solution.py:310
  48.7 0.0 copy-start
  48.8 2.3 %convert_bitcast_fusion = (f32[1024,153]{0,1:T(8,128)}, f32[1024,153]{0,1:T(8,128)}) fusion(bf16[320,1024]{1,0:T(8,128)(2,1)} %get-tuple-element.6), kind=kLoop, calls=%fused_computation | loop fusion | flops 313344 | bytes 1880064 | tf_op jit(solution)/shard_map/transpose | solution.py:369
  51.1 0.0 copy-done
  51.1 0.6 %copy.19 = f32[1,128,153]{1,0,2:T(1,128)} copy(f32[1,128,153]{1,0,2:T(1,128)S(1)} %bitcast.22) | data formatting | bytes 156672
Async XLA Ops:
  48.7 2.3 %copy-start = (f32[153,1,128]{2,1,0:T(1,128)S(1)}, f32[153,1,128]{2,1,0:T(1,128)}, u32[]{:S(2)}) copy-start(f32[153,1,128]{2,1,0:T(1,128)} %get-tuple-element.5) | copy-start | bytes 235012

commit v3 on v2

--- a/solution.py
+++ b/solution.py
@@ -109,7 +109,7 @@
     tile1, tile2 = dst1.shape[0], dst2.shape[0]
     per = words1.shape[0] // tile1
     cp = cotg.shape[1]
-    pc = gsend.shape[1]
+    halves, _, pc, hw = gsend.shape
     zs = partners(z, nz)
     qs = partners(q, planes)
 
@@ -178,11 +178,12 @@
         term = dot(feats[:, k : k + chunk], onehot, NN)
         self_t = term if self_t is None else self_t + term
     self_t = self_t.astype(BF16)
-    for j in range(nz):
-        cols = slice(j * hc, (j + 1) * hc)
-        part[j] = (dot(self_t, w1s[:, cols], TN) + dot(mean_t, w1n[:, cols], TN)).astype(BF16)
-    for p in zs:
-        send(part.at[p], got.at[z], part_s.at[p], part_r.at[z], at(p, q))
+    for h in range(halves):
+        for j in range(nz):
+            cols = slice(j * hc + h * hw, j * hc + (h + 1) * hw)
+            part[h, j] = (dot(self_t, w1s[:, cols], TN) + dot(mean_t, w1n[:, cols], TN)).astype(BF16)
+        for p in zs:
+            send(part.at[h, p], got.at[h, z], part_s.at[h, p], part_r.at[h, z], at(p, q))
 
     for t in range(tile2):
         masks2[t] = unpack([words2[t * per + k] for k in range(per)], row_word, row_shift)
@@ -221,52 +222,66 @@
     if cg.shape[0] > 2 * cp:
         cg[2 * cp :, :] = jnp.zeros((cg.shape[0] - 2 * cp, nodes), BF16)
 
-    summed = part[z].astype(F32) + bias
-    for p in zs:
-        arrived(got.at[p], part_s.at[p], part_r.at[p], at(p, q))
-        summed = summed + got[p].astype(F32)
-    hidden = jnp.maximum(summed, 0.0).astype(BF16)
-
-    grads = dot(cg[...], hidden, NN).astype(BF16)
-    for p in range(planes):
-        gsend[p] = grads[p * pc : (p + 1) * pc, :]
-    for p in qs:
-        send(gsend.at[p], ggot.at[q], g_s.at[p], g_r.at[q], at(z, p))
-
-    uv = dot(w2, hidden, NT)
+    ds = partners(d, nd)
+    rs = partners(r, nr)
+
+    def multiply(h):
+        cols = slice(h * hw, (h + 1) * hw)
+        summed = part[h, z].astype(F32) + bias[:, cols]
+        for p in zs:
+            arrived(got.at[h, p], part_s.at[h, p], part_r.at[h, p], at(p, q))
+            summed = summed + got[h, p].astype(F32)
+        hidden = jnp.maximum(summed, 0.0).astype(BF16)
+        grads = dot(cg[...], hidden, NN).astype(BF16)
+        for p in range(planes):
+            gsend[h, p] = grads[p * pc : (p + 1) * pc, :]
+        for p in qs:
+            send(gsend.at[h, p], ggot.at[h, q], g_s.at[h, p], g_r.at[h, q], at(z, p))
+        return dot(w2[:, cols], hidden, NT)
+
+    def add_slots(h):
+        total = gsend[h, q].astype(F32)
+        for p in qs:
+            arrived(ggot.at[h, p], g_s.at[h, p], g_r.at[h, p], at(z, p))
+            total = total + ggot[h, p].astype(F32)
+        full[h, z, q] = total.astype(BF16)
+        for p in zs:
+            send(full.at[h, z, q], full.at[h, z, q], z_s.at[h, p], z_r.at[h, z], at(p, q))
+
+    def to_core(h, zz, dd):
+        piece = full.at[h, zz, dd * nr + r]
+        for p in rs:
+            send(piece, piece, c_s.at[h, zz, dd, p], c_r.at[h, zz, dd, r], (y, z, d, p))
+
+    def pass_on(h):
+        for zz in [z] + zs[::-1]:
+            piece = full.at[h, zz, q]
+            if zz is not z:
+                arrived(piece, z_s.at[h, zz], z_r.at[h, zz], at(zz, q))
+            for p in ds:
+                send(piece, piece, x_s.at[h, zz, p], x_r.at[h, zz, d], (y, z, p, r))
+            to_core(h, zz, d)
+
+    def pass_cores(h):
+        for zz in [z] + zs[::-1]:
+            for p in ds:
+                arrived(full.at[h, zz, p * nr + r], x_s.at[h, zz, p], x_r.at[h, zz, p], (y, z, p, r))
+                to_core(h, zz, p)
+
+    uv = multiply(0)
+    for h in range(1, halves):
+        add_slots(h - 1)
+        uv = uv + multiply(h)
     lf[...] = uv[0:cp, :] + dot(uv[cp:, :].astype(BF16), adj2[...], NT) * inverse2
     for j in range(nz):
         lsend[j] = lf[:, j * BLK : (j + 1) * BLK].astype(BF16)
-
-    total = gsend[q].astype(F32)
-    for p in qs:
-        arrived(ggot.at[p], g_s.at[p], g_r.at[p], at(z, p))
-        total = total + ggot[p].astype(F32)
-    full[z, q] = total.astype(BF16)
-    for p in zs:
-        send(full.at[z, q], full.at[z, q], z_s.at[p], z_r.at[z], at(p, q))
     for p in zs:
         send(lsend.at[p], lgot.at[z], l_s.at[p], l_r.at[z], at(p, q))
-
-    ds = partners(d, nd)
-    rs = partners(r, nr)
-
-    def to_core(zz, dd):
-        piece = full.at[zz, dd * nr + r]
-        for p in rs:
-            send(piece, piece, c_s.at[zz, dd, p], c_r.at[zz, dd, r], (y, z, d, p))
-
-    for zz in [z] + zs[::-1]:
-        piece = full.at[zz, q]
-        if zz is not z:
-            arrived(piece, z_s.at[zz], z_r.at[zz], at(zz, q))
-        for p in ds:
-            send(piece, piece, x_s.at[zz, p], x_r.at[zz, d], (y, z, p, r))
-        to_core(zz, d)
-    for zz in [z] + zs[::-1]:
-        for p in ds:
-            arrived(full.at[zz, p * nr + r], x_s.at[zz, p], x_r.at[zz, p], (y, z, p, r))
-            to_core(zz, p)
+    add_slots(halves - 1)
+    for h in range(halves):
+        pass_on(h)
+    for h in range(halves):
+        pass_cores(h)
 
     out = lf[:, pl.ds(pl.multiple_of(z * BLK, BLK), BLK)]
     for p in zs:
@@ -276,13 +291,16 @@
     bias_two = jnp.broadcast_to(b2[...], (BLK, classes)).T
     logits_out[:, 0, :] = wide[0:classes, :] + bias_two
 
-    for zz in range(nz):
-        for dd in range(nd):
-            for p in rs:
-                arrived(full.at[zz, dd * nr + p], c_s.at[zz, dd, p], c_r.at[zz, dd, p], (y, z, d, p))
-    for zz in range(nz):
-        for p in range(planes):
-            grads_out[p * pc : (p + 1) * pc, zz * hc : (zz + 1) * hc] = full[zz, p]
+    for h in range(halves):
+        for zz in range(nz):
+            for dd in range(nd):
+                for p in rs:
+                    arrived(
+                        full.at[h, zz, dd * nr + p], c_s.at[h, zz, dd, p], c_r.at[h, zz, dd, p], (y, z, d, p)
+                    )
+            for p in range(planes):
+                first = zz * hc + h * hw
+                grads_out[p * pc : (p + 1) * pc, first : first + hw] = full[h, zz, p]
     for copy in pending:
         copy.wait_send()
 
@@ -299,6 +317,8 @@
     cp = round_up(classes, 16)
     rows = round_up(2 * cp, 16 * planes)
     pc = rows // planes
+    halves = 1 if hc % (2 * BLK) else 2
+    hw = hc // halves
     cot = cotangent.transpose(2, 0, 1)
     w2s, w2n, b1 = w2_self.T, w2_neigh.T, bias_one[None, :]
     if hc % BLK:
@@ -319,30 +339,30 @@
             pltpu.VMEM((tile2, BLK, BLK), F32),
             pltpu.VMEM((nodes, tile1 * BLK), BF16),
             pltpu.VMEM((nodes, nodes), BF16),
-            pltpu.VMEM((nz, nodes, hc), BF16),
-            pltpu.VMEM((nz, nodes, hc), BF16),
+            pltpu.VMEM((halves, nz, nodes, hw), BF16),
+            pltpu.VMEM((halves, nz, nodes, hw), BF16),
             pltpu.VMEM((2 * cp, hc), F32),
             pltpu.VMEM((cp, nodes), F32),
             pltpu.VMEM((nz, cp, BLK), BF16),
             pltpu.VMEM((nz, cp, BLK), BF16),
             pltpu.VMEM((rows, nodes), BF16),
-            pltpu.VMEM((planes, pc, hc), BF16),
-            pltpu.VMEM((planes, pc, hc), BF16),
-            pltpu.VMEM((nz, planes, pc, hc), BF16),
+            pltpu.VMEM((halves, planes, pc, hw), BF16),
+            pltpu.VMEM((halves, planes, pc, hw), BF16),
+            pltpu.VMEM((halves, nz, planes, pc, hw), BF16),
             dma((nz,)),
             dma((nz,)),
+            dma((halves, nz)),
+            dma((halves, nz)),
             dma((nz,)),
             dma((nz,)),
-            dma((nz,)),
-            dma((nz,)),
-            dma((planes,)),
-            dma((planes,)),
-            dma((nz,)),
-            dma((nz,)),
-            dma((nz, nd)),
-            dma((nz, nd)),
-            dma((nz, nd, nr)),
-            dma((nz, nd, nr)),
+            dma((halves, planes)),
+            dma((halves, planes)),
+            dma((halves, nz)),
+            dma((halves, nz)),
+            dma((halves, nz, nd)),
+            dma((halves, nz, nd)),
+            dma((halves, nz, nd, nr)),
+            dma((halves, nz, nd, nr)),
         ],
         compiler_params=pltpu.CompilerParams(
             collective_id=0, has_side_effects=True, vmem_limit_bytes=60 * 1024 * 1024

time: 52.3 us -> 51.8 us (level)
  no operation moved by 1% of the time
where the time goes in v3:
time: 51.8 us; the launch traced here: 51.6 us
  Pallas kernels  48 us (93%)
  other arithmetic  2.3 us (4%)
  between operations  0.65 us (1%)
  local copies, waits for them, and re-layouts  0.64 us (1%)
    pallas_call x1, Pallas kernels, body(): pl.pallas_call(functools.partial(kernel, (nz, nd, nr, hc, classes)), out_...  48 us
    transpose x1, other arithmetic, body(): grad_neigh = grads[cp:cp + classes].astype(F32).T  2.3 us

profile of v3, /device:TPU:0, one launch (start us, length us, event | category | flops | bytes accessed | tf_op | source)
XLA Modules:
  0.0 51.6 jit_solution(12306182547868642580)
XLA Ops:
  0.6 48.0 %shard_map.166 = (f32[153,1,128]{2,1,0:T(1,128)}, bf16[320,1024]{1,0:T(8,128)(2,1)}) custom-call(s32[6]{0:T(128)} %bitcast.28, s32[6]{0:T(128)} %bitcast.29, s32[5]{0:T(128)} %bitcast.30, s32[5]{0:T(128)} %bitcast.31, s32[1,512]{1,0:T(1,128)} %ids.1, s32[30,1,128]{2,1,0:T(1,128)} %bitcast.24, s32[25,1,128]{2,1,0:T(1,128)} %bitcast.25, ...), custom_call_target="tpu_custom_call" | custom-call | tf_op jit(solution)/shard_map/pallas_call | solution.py:330
  48.7 0.0 copy-start
  48.7 2.3 %convert_bitcast_fusion = (f32[1024,153]{0,1:T(8,128)}, f32[1024,153]{0,1:T(8,128)}) fusion(bf16[320,1024]{1,0:T(8,128)(2,1)} %get-tuple-element.6), kind=kLoop, calls=%fused_computation | loop fusion | flops 313344 | bytes 1880064 | tf_op jit(solution)/shard_map/transpose | solution.py:389
  51.0 0.0 copy-done
  51.0 0.6 %copy.19 = f32[1,128,153]{1,0,2:T(1,128)} copy(f32[1,128,153]{1,0,2:T(1,128)S(1)} %bitcast.22) | data formatting | bytes 156672
Async XLA Ops:
  48.7 2.3 %copy-start = (f32[153,1,128]{2,1,0:T(1,128)S(1)}, f32[153,1,128]{2,1,0:T(1,128)}, u32[]{:S(2)}) copy-start(f32[153,1,128]{2,1,0:T(1,128)} %get-tuple-element.5) | copy-start | bytes 235012
